TPU v7x, 32 devices: a whole 2x2x4 slice. The times are simulated.
32 devices in a mesh: groups: 2 (over x), gx: 8 (over z, y), gy: 2 (over core).
Axes of the slice: x: 2, y: 2, z: 4, core: 2. Of those that a mesh axis runs over, the one named last changes fastest.
Arguments:
- hidden_state_rows: bfloat16 [384, 16384], P(('groups', 'gx'), 'gy'), parts along dimension 0, may hold values from -6 to 6
- base_projection_weight: bfloat16 [16384, 16384], P('gx', 'gy'), may hold values from -0.046875 to 0.046875
- adapter_down_weight: bfloat16 [16384, 64, 16], P('gy', 'gx'), may hold values from -0.046875 to 0.046875
- adapter_up_weight: bfloat16 [64, 16, 16384], P('gx', None, 'gy'), may hold values from -1.5 to 1.5
- adapter_index_rows: int32 [384], P(('groups', 'gx')), parts along dimension 0, may hold values from 0 to 63, as said below
Outputs:
- projected: bfloat16 [384, 16384], P(('groups', 'gx'), 'gy'), parts along dimension 0
There are 2 independent parts, one for each index of `groups`. A program takes and returns all parts, laid end to end along the dimension named above; an argument that names none is the same for every part. Nothing has to cross between parts.
Inputs may be any that keep to these rules, and one draw needn't show every extreme that they name: `adapter_index_rows`: adapter a belongs to owner a // 8. In each aligned block of 24 rows, no owner's adapters are named by more than 6 rows, and in every block some owner's adapters are named by exactly 6 rows.
All inputs are finite; a program needn't handle non-finite values.
Results may differ from a plain program's by a relative error of at most 0.014.
Values may be sent and summed in bfloat16 or wider, within the bound.
A program may use at most 128 MiB of HBM per device.

v0:
```python
import jax
import jax.numpy as jnp
from jax import lax
from jax.sharding import PartitionSpec as P

UPDATE_SCALE = 0.5


def on_device(
    hidden_state_rows,
    base_projection_weight,
    adapter_down_weight,
    adapter_up_weight,
    adapter_index_rows,
):
    row_dev = hidden_state_rows.shape[0]
    width_halved = hidden_state_rows.shape[1]
    adapter_per_chip_set = adapter_up_weight.shape[0]
    rank_width_total = adapter_up_weight.shape[1]
    down_joined_weight = adapter_down_weight.reshape(
        width_halved, adapter_per_chip_set * rank_width_total
    )
    up_joined_weight = adapter_up_weight.reshape(
        adapter_per_chip_set * rank_width_total, width_halved
    )
    first_adapter = lax.axis_index("gx") * adapter_per_chip_set
    column_group = (
        jnp.arange(adapter_per_chip_set * rank_width_total, dtype=jnp.int32) // rank_width_total
    )
    full_rows = lax.all_gather(hidden_state_rows, "gy", axis=1, tiled=True)
    tile_rows = lax.all_to_all(full_rows, "gx", split_axis=1, concat_axis=0, tiled=True)
    owner_count = lax.axis_size("gx")
    capacity = max(2, 2 * row_dev // owner_count)
    slot_total = owner_count * capacity
    owners = adapter_index_rows // adapter_per_chip_set
    position = jnp.arange(row_dev, dtype=jnp.int32)
    earlier = (owners[None, :] == owners[:, None]) & (position[None, :] < position[:, None])
    slot_rank = jnp.sum(earlier.astype(jnp.int32), axis=1)
    slot_index = owners * capacity + slot_rank
    placing = slot_index[None, :] == jnp.arange(slot_total, dtype=jnp.int32)[:, None]
    placer = placing.astype(jnp.bfloat16)
    packed = jnp.dot(placer, hidden_state_rows, preferred_element_type=jnp.float32).astype(
        jnp.bfloat16
    )
    packed = packed.reshape(owner_count, capacity, width_halved)
    slot_ids = jnp.sum(jnp.where(placing, adapter_index_rows[None, :] + 1, 0), axis=1) - 1
    slot_ids = slot_ids.reshape(owner_count, capacity)
    slot_place = jnp.sum(jnp.where(placing, position[None, :] + 1, 0), axis=1) - 1
    slot_place = slot_place.reshape(owner_count, capacity)
    payload = (packed, slot_ids, slot_place)
    rows_in = lax.all_to_all(payload[0], "gx", split_axis=0, concat_axis=0, tiled=True)
    ids_in = lax.all_to_all(payload[1], "gx", split_axis=0, concat_axis=0, tiled=True)
    source_count = rows_in.shape[0]
    item_count = rows_in.shape[1]
    flat_rows = rows_in.reshape(source_count * item_count, width_halved)
    totals = lax.psum(
        jnp.dot(flat_rows, down_joined_weight, preferred_element_type=jnp.float32).astype(
            jnp.bfloat16
        ),
        "gy",
    ).astype(jnp.float32)
    local_index = ids_in.reshape(source_count * item_count) - first_adapter
    matches = column_group[None, :] == local_index[:, None]
    reduced_rank_rows = jnp.where(matches, totals, 0.0).astype(jnp.bfloat16)
    update_block_local = (
        UPDATE_SCALE
        * jnp.dot(reduced_rank_rows, up_joined_weight, preferred_element_type=jnp.float32)
    ).astype(jnp.bfloat16)
    update_block_local = update_block_local.reshape(source_count, item_count, width_halved)
    place_held = lax.all_to_all(payload[2], "gx", split_axis=0, concat_axis=0, tiled=True)
    source_count = update_block_local.shape[0]
    item_count = update_block_local.shape[1]
    delta_flat = update_block_local.reshape(source_count * item_count, width_halved)
    source_first = jnp.arange(source_count, dtype=jnp.int32)[:, None] * row_dev
    target = jnp.where(place_held >= 0, source_first + place_held, -1).reshape(
        source_count * item_count
    )
    row_numbers = jnp.arange(row_dev * lax.axis_size("gx"), dtype=jnp.int32)
    hits = (target[None, :] == row_numbers[:, None]).astype(jnp.bfloat16)
    partial_sum = jnp.dot(
        tile_rows, base_projection_weight, preferred_element_type=jnp.float32
    ).astype(jnp.bfloat16)
    return lax.psum_scatter(
        (
            lax.optimization_barrier(partial_sum).astype(jnp.float32)
            + jnp.dot(hits, delta_flat, preferred_element_type=jnp.float32)
        ).astype(jnp.bfloat16),
        "gx",
        scatter_dimension=0,
        tiled=True,
    )


def solution(mesh):
    return jax.shard_map(
        on_device,
        mesh=mesh,
        in_specs=(
            P(("groups", "gx"), "gy"),
            P("gx", "gy"),
            P("gy", "gx", None),
            P("gx", None, "gy"),
            P(("groups", "gx")),
        ),
        out_specs=P(("groups", "gx"), "gy"),
        check_vma=False,
    )
```

profile of v0, /device:TPU:0, one launch (start us, length us, event | category | flops | bytes accessed | tf_op | source)
XLA Modules:
  0.0 183.2 jit_solution(2931629300357551492)
XLA Ops:
  6.5 0.8 and_select_fusion.1
  7.4 0.2 convert_reduce_fusion
  7.7 0.7 sub.35
  8.3 7.3 %all-to-all-start.1 = ((s32[8,1,6]{2,1,0:T(1,128)}), s32[8,1,6]{2,1,0:T(1,128)S(1)}, u32[]{:S(2)}, u32[]{:S(2)}) async-start(s32[8,1,6]{2,1,0:T(1,128)} %bitcast.2), calls=%async_computation.1 | async-start | bytes 8192 | tf_op jit(solution)/shard_map/all_to_all | solution.py:70
  15.6 0.7 sub.38
  16.3 5.7 %all-to-all-done.1 = s32[8,1,6]{2,1,0:T(1,128)S(1)} async-done(((s32[8,1,6]{2,1,0:T(1,128)}), s32[8,1,6]{2,1,0:T(1,128)S(1)}, u32[]{:S(2)}, u32[]{:S(2)}) %all-to-all-start.1) | async-done | bytes 224 | tf_op jit(solution)/shard_map/all_to_all | solution.py:70
  22.0 3.3 %all-to-all-start.2 = ((s32[8,1,6]{2,1,0:T(1,128)}), s32[8,1,6]{2,1,0:T(1,128)S(1)}, u32[]{:S(2)}, u32[]{:S(2)}) async-start(s32[8,1,6]{2,1,0:T(1,128)} %bitcast.3), calls=%async_computation.2 | async-start | bytes 8192 | tf_op jit(solution)/shard_map/all_to_all | solution.py:52
  25.3 1.5 convolution_convert_fusion.1
  26.8 1.3 reshape.100
  28.1 3.6 %all-to-all-done.2 = s32[8,1,6]{2,1,0:T(1,128)S(1)} async-done(((s32[8,1,6]{2,1,0:T(1,128)}), s32[8,1,6]{2,1,0:T(1,128)S(1)}, u32[]{:S(2)}, u32[]{:S(2)}) %all-to-all-start.2) | async-done | bytes 224 | tf_op jit(solution)/shard_map/all_to_all | solution.py:52
  31.7 3.6 %all-to-all-start.3 = ((bf16[8,6,8192]{2,1,0:T(8,128)(2,1)}), bf16[8,6,8192]{2,1,0:T(8,128)(2,1)S(1)}, u32[]{:S(2)}, u32[]{:S(2)}) async-start(bf16[8,6,8192]{2,1,0:T(8,128)(2,1)} %reshape.100), calls=%async_computation.3 | async-start | bytes 2097152 | tf_op jit(solution)/shard_map/all_to_all | solution.py:51
  35.3 2.4 %all_gather.3 = bf16[24,16384]{1,0:T(8,128)(2,1)S(1)} all-gather(bf16[24,8192]{1,0:T(8,128)(2,1)S(1)} %copy-done.1), channel_id=1, replica_groups=mesh['groups'=2,'gx'=8,'gy'=2] {'gy'}, dimensions={1}, use_global_device_ids=true | all-gather | bytes 1179648 | tf_op jit(solution)/shard_map/all_gather | solution.py:30
  37.7 1.0 copy.15
  38.7 20.2 %all-to-all-done.3 = bf16[8,6,8192]{2,1,0:T(8,128)(2,1)S(1)} async-done(((bf16[8,6,8192]{2,1,0:T(8,128)(2,1)}), bf16[8,6,8192]{2,1,0:T(8,128)(2,1)S(1)}, u32[]{:S(2)}, u32[]{:S(2)}) %all-to-all-start.3) | async-done | bytes 786464 | tf_op jit(solution)/shard_map/all_to_all | solution.py:51
  58.9 4.2 %all-to-all-start = ((bf16[24,8,2048]{2,0,1:T(8,128)(2,1)}), bf16[24,8,2048]{2,0,1:T(8,128)(2,1)}, u32[]{:S(2)}, u32[]{:S(2)}) async-start(bf16[24,8,2048]{2,0,1:T(8,128)(2,1)} %bitcast.18), calls=%async_computation | async-start | bytes 1572864 | tf_op jit(solution)/shard_map/all_to_all | solution.py:31
  63.3 0.5 broadcast.126
  63.8 0.7 reduce.7
  64.7 1.2 reshape.101
  65.9 2.7 %convolution_convert_fusion.2 = bf16[48,128]{1,0:T(8,128)(2,1)S(1)} fusion(bf16[48,8192]{1,0:T(8,128)(2,1)} %reshape.101, bf16[8192,128]{0,1:T(8,128)(2,1)} %bitcast.20), kind=kOutput, calls=%fused_computation.6 | convolution fusion | flops 100669440 | bytes 2895872 | tf_op jit(solution)/shard_map/dot_general | solution.py:57
  68.5 3.3 %psum.7 = bf16[48,128]{1,0:T(8,128)(2,1)S(1)} all-reduce(bf16[48,128]{1,0:T(8,128)(2,1)S(1)} %convolution_convert_fusion.2), channel_id=1, replica_groups=mesh['groups'=2,'gx'=8,'gy'=2] {'gy'}, use_global_device_ids=true, to_apply=%region_3.4 | all-reduce | flops 6144 | bytes 24576 | tf_op jit(solution)/shard_map/psum | solution.py:56
  71.8 10.2 %all-to-all-done = bf16[24,8,2048]{2,0,1:T(8,128)(2,1)} async-done(((bf16[24,8,2048]{2,0,1:T(8,128)(2,1)}), bf16[24,8,2048]{2,0,1:T(8,128)(2,1)}, u32[]{:S(2)}, u32[]{:S(2)}) %all-to-all-start) | async-done | bytes 786464 | tf_op jit(solution)/shard_map/all_to_all | solution.py:31
  82.0 16.0 %convolution_convert_fusion = bf16[192,8192]{1,0:T(8,128)(2,1)} fusion(bf16[192,2048]{1,0:T(8,128)(2,1)} %bitcast.1, bf16[2048,8192]{1,0:T(8,128)(2,1)} %param.6), kind=kOutput, calls=%fused_computation.2 | convolution fusion | flops 6444023808 | bytes 37486592 | tf_op jit(solution)/shard_map/dot_general | solution.py:80
  98.0 4.8 %fusion = bf16[192,8192]{1,0:T(8,128)(2,1)} fusion(bf16[192,8192]{1,0:T(8,128)(2,1)} %convolution_convert_fusion, bf16[128,8192]{1,0:T(8,128)(2,1)S(1)} %bitcast.17, s32[48]{0:T(128)S(1)} %compare_select_fusion, bf16[48,128]{1,0:T(8,128)(2,1)S(1)} %psum.7, s32[128]{0:T(128)S(1)} %and_select_fusion, s32[48]{0:T(128)S(1)} %sub.41), kind=kOutput, calls=%fused_computation.1 | convolution fusion | flops 257197056 | bytes 8401792 | tf_op jit(solution)/shard_map/dot_general | solution.py:86
  102.8 73.5 %reduce-scatter.2.cloned.1.call-done = bf16[24,8192]{1,0:T(8,128)(2,1)} async-done(((bf16[192,8192]{1,0:T(8,128)(2,1)}), bf16[24,8192]{1,0:T(8,128)(2,1)}) %reduce-scatter.2.cloned.1.call-update) | async-done | bytes 393232 | tf_op jit(solution)/shard_map/reduce_scatter | solution.py:83
  (18 shorter events, 0.5 us)
Async XLA Ops:
  6.5 91.4 %copy-start = (bf16[8,16,8192]{2,1,0:T(8,128)(2,1)S(1)}, bf16[8,16,8192]{2,1,0:T(8,128)(2,1)}, u32[]{:S(2)}) copy-start(bf16[8,16,8192]{2,1,0:T(8,128)(2,1)} %param.8) | copy-start | bytes 6291460
  6.5 28.8 %copy-start.1 = (bf16[24,8192]{1,0:T(8,128)(2,1)S(1)}, bf16[24,8192]{1,0:T(8,128)(2,1)}, u32[]{:S(2)}) copy-start(bf16[24,8192]{1,0:T(8,128)(2,1)} %param.5) | copy-start | bytes 1179652
  8.3 13.7 %all-to-all-start.1 = ((s32[8,1,6]{2,1,0:T(1,128)}), s32[8,1,6]{2,1,0:T(1,128)S(1)}, u32[]{:S(2)}, u32[]{:S(2)}) async-start(s32[8,1,6]{2,1,0:T(1,128)} %bitcast.2), calls=%async_computation.1 | async-start | bytes 8192 | tf_op jit(solution)/shard_map/all_to_all | solution.py:70
  22.0 9.7 %all-to-all-start.2 = ((s32[8,1,6]{2,1,0:T(1,128)}), s32[8,1,6]{2,1,0:T(1,128)S(1)}, u32[]{:S(2)}, u32[]{:S(2)}) async-start(s32[8,1,6]{2,1,0:T(1,128)} %bitcast.3), calls=%async_computation.2 | async-start | bytes 8192 | tf_op jit(solution)/shard_map/all_to_all | solution.py:52
  31.7 27.1 %all-to-all-start.3 = ((bf16[8,6,8192]{2,1,0:T(8,128)(2,1)}), bf16[8,6,8192]{2,1,0:T(8,128)(2,1)S(1)}, u32[]{:S(2)}, u32[]{:S(2)}) async-start(bf16[8,6,8192]{2,1,0:T(8,128)(2,1)} %reshape.100), calls=%async_computation.3 | async-start | bytes 2097152 | tf_op jit(solution)/shard_map/all_to_all | solution.py:51
  58.9 23.1 %all-to-all-start = ((bf16[24,8,2048]{2,0,1:T(8,128)(2,1)}), bf16[24,8,2048]{2,0,1:T(8,128)(2,1)}, u32[]{:S(2)}, u32[]{:S(2)}) async-start(bf16[24,8,2048]{2,0,1:T(8,128)(2,1)} %bitcast.18), calls=%async_computation | async-start | bytes 1572864 | tf_op jit(solution)/shard_map/all_to_all | solution.py:31
  63.1 113.2 %reduce-scatter.2.cloned.1.call-start = ((), (), s32[]{:S(2)}) async-start(), calls=%async_computation.5 | async-start | bytes 3538944 | tf_op jit(solution)/shard_map/reduce_scatter | solution.py:83
Sparse Core Ops, SparseCore 0:
  102.9 73.3 reduce-scatter.1
where the time goes:
time: 184 us; the launch traced here: 183 us
  waiting for transfers between devices  113 us (61%)
  matrix products  24.9 us (14%)
  starting transfers between devices  18.4 us (10%)
  between operations  13.5 us (7%)
  blocking collectives  5.66 us (3%)
  local copies, waits for them, and re-layouts  5.63 us (3%)
    reduce_scatter x1, waiting for transfers between devices, on_device(): lax.psum_scatter((lax.optimization_barrier(partial_sum).astype(jnp.float3...  73.5 us
    all_to_all x1, waiting for transfers between devices, on_device(): lax.all_to_all(payload[0], 'gx', split_axis=0, concat_axis=0, tiled=True)  20.2 us
    dot_general x1, matrix products, on_device(): jnp.dot(tile_rows, base_projection_weight, preferred_element_type=jnp.flo...  16 us
    all_to_all x1, waiting for transfers between devices, on_device(): lax.all_to_all(full_rows, 'gx', split_axis=1, concat_axis=0, tiled=True)  10.2 us
    all_to_all x1, starting transfers between devices, on_device(): lax.all_to_all(payload[2], 'gx', split_axis=0, concat_axis=0, tiled=True)  7.28 us
    all_to_all x1, waiting for transfers between devices, on_device(): lax.all_to_all(payload[2], 'gx', split_axis=0, concat_axis=0, tiled=True)  5.72 us
    dot_general x1, matrix products, on_device(): jnp.dot(hits, delta_flat, preferred_element_type=jnp.float32)  4.84 us
    all_to_all x1, starting transfers between devices, on_device(): lax.all_to_all(full_rows, 'gx', split_axis=1, concat_axis=0, tiled=True)  4.21 us
  transfers between devices with their start and end apart: 5, of which 5 were waited for; matrix products, arithmetic and copies ran while one was open for 5% of the time, Pallas kernels for 0%

commit v1 on v0

v1 whole, which is shorter than its diff:
```python
import functools

import jax
import jax.numpy as jnp
from jax import lax
from jax.experimental import pallas as pl
from jax.experimental.pallas import tpu as pltpu
from jax.sharding import PartitionSpec as P

UPDATE_SCALE = 0.5
FOLD = 8
ROW_PAD = 32
MESH = pl.DeviceIdType.MESH
F32 = jnp.float32
BF16 = jnp.bfloat16


def kernel(
    n, capacity, rank, chunks,
    ids_ref, hid_ref, w_ref, down_ref, up_ref, out_ref,
    w_v, down_v, up_v, ids_all, tile_in, rows, folded, packed, slots_in,
    half_out, half_in, part, y_in, z_in,
    w_sem, ad_sem, id_send, id_recv, t_send, t_recv, f_send, l_send, l_recv,
    h_send, h_recv, y_send, y_recv, z_send, z_recv,
):
    g, c, s = lax.axis_index("groups"), lax.axis_index("gx"), lax.axis_index("gy")
    m = n // 2
    zz, yy = c // 2, c % 2
    row_dev, width = hid_ref.shape
    tile = w_ref.shape[0]
    fold_width = width // FOLD
    slot_rows = capacity * FOLD
    cc = width // chunks
    primary = (c // m) == s

    def peer(cx):
        return (g, cx, s)

    partner = (g, c, 1 - s)

    def w_copy(k):
        cols = pl.ds(pl.multiple_of(k * cc, cc), cc)
        return pltpu.make_async_copy(w_ref.at[:, cols], w_v.at[:, cols], w_sem.at[k])

    down_copy = pltpu.make_async_copy(down_ref, down_v, ad_sem.at[0])
    up_copy = pltpu.make_async_copy(up_ref, up_v, ad_sem.at[1])

    barrier = pltpu.get_barrier_semaphore()
    for j in range(1, n):
        pl.semaphore_signal(barrier, inc=1, device_id=peer((c + j) % n), device_id_type=MESH)
    pl.semaphore_signal(barrier, inc=1, device_id=partner, device_id_type=MESH)

    @pl.loop(0, chunks)
    def _(k):
        w_copy(k).start()

    down_copy.start()
    up_copy.start()

    pl.semaphore_wait(barrier, n)

    def id_copy(dst, j):
        return pltpu.make_async_remote_copy(
            ids_ref, ids_all.at[c], id_send.at[j], id_recv.at[c], device_id=peer(dst),
            device_id_type=MESH,
        )

    def tile_copy(j):
        t = s * m + j
        cols = pl.ds(pl.multiple_of(j * tile, tile), tile)
        return t, pltpu.make_async_remote_copy(
            hid_ref.at[:, cols], tile_in.at[c], t_send.at[j], t_recv.at[c],
            device_id=peer(t), device_id_type=MESH,
        )

    own_cols = pl.ds(pl.multiple_of((c - s * m) * tile, tile), tile)

    @pl.loop(0, m)
    def _(j):
        t, copy = tile_copy(j)

        @pl.when(t != c)
        def _():
            copy.start()

    @pl.when(primary)
    def _():
        pltpu.make_async_copy(hid_ref.at[:, own_cols], tile_in.at[c], t_recv.at[c]).start()

    @pl.loop(1, n)
    def _(j):
        id_copy((c + j) % n, j).start()

    own_ids = pltpu.make_async_copy(ids_ref, ids_all.at[c], id_recv.at[c])
    own_ids.start()

    k_pad = FOLD * ROW_PAD
    owner_row = ids_ref[1:2, :]
    lane = lax.broadcasted_iota(jnp.int32, (ROW_PAD, k_pad), 1)
    sub = lax.broadcasted_iota(jnp.int32, (ROW_PAD, k_pad), 0)
    owner_all = jnp.broadcast_to(owner_row, (ROW_PAD, k_pad))
    owner_col = jnp.sum(jnp.where(lane == sub, owner_all, 0.0), axis=1, keepdims=True)
    earlier = (owner_all == owner_col) & (sub < (lane & (ROW_PAD - 1)))
    rank_row = jnp.sum(jnp.where(earlier, 1.0, 0.0), axis=0, keepdims=True)
    code_row = jnp.where(owner_row >= 0.0, owner_row * capacity + rank_row, -1.0)
    code_row = code_row.astype(jnp.int32)
    total_rows = n * slot_rows
    big_row = lax.broadcasted_iota(jnp.int32, (total_rows, k_pad), 0)
    big_lane = lax.broadcasted_iota(jnp.int32, (total_rows, k_pad), 1)
    placer = ((big_row >> 3) == code_row) & ((big_row & 7) == (big_lane >> 5))
    placer = jnp.where(placer, 1.0, 0.0).astype(BF16)
    for q in range(FOLD):
        block = hid_ref[:, q * fold_width:(q + 1) * fold_width].astype(F32)
        block = jnp.concatenate(
            [block, jnp.zeros((ROW_PAD - row_dev, fold_width), F32)], axis=0
        )
        folded[q * ROW_PAD:(q + 1) * ROW_PAD, :] = block.astype(BF16)
    sent = jnp.dot(placer, folded[...], preferred_element_type=F32).astype(BF16)
    for d in range(n):
        packed[d] = sent[d * slot_rows:(d + 1) * slot_rows, :]

    def slot_copy(dst, j):
        return pltpu.make_async_remote_copy(
            packed.at[dst], slots_in.at[c], l_send.at[j], l_recv.at[c], device_id=peer(dst),
            device_id_type=MESH,
        )

    @pl.loop(1, n)
    def _(j):
        slot_copy((c + j) % n, j).start()

    own_slots = pltpu.make_async_copy(packed.at[c], slots_in.at[c], l_recv.at[c])
    own_slots.start()

    def forward(src):
        return pltpu.make_async_remote_copy(
            tile_in.at[src], tile_in.at[src], f_send.at[src], t_recv.at[src],
            device_id=partner, device_id_type=MESH,
        )

    @pl.loop(0, n)
    def _(j):
        src = (c + j) % n
        forward(src).wait_recv()

        @pl.when(primary)
        def _():
            forward(src).start()

    for p in range(m):
        pair = jnp.concatenate([tile_in[2 * p].astype(F32), tile_in[2 * p + 1].astype(F32)], axis=0)
        rows[2 * row_dev * p:2 * row_dev * (p + 1), :] = pair.astype(BF16)

    def columns(k):
        return pl.ds(pl.multiple_of(k * cc, cc), cc)

    @pl.loop(0, chunks)
    def _(k):
        w_copy(k).wait()
        cols = columns(k)
        acc = jnp.dot(rows[...], w_v[:, cols], preferred_element_type=F32)
        for b in range(n):
            part[b % 2, b // 2, :, cols] = acc[b * row_dev:(b + 1) * row_dev, :].astype(BF16)

    @pl.loop(1, n)
    def _(j):
        src = (c + j) % n
        pltpu.make_async_remote_copy(
            packed.at[src], slots_in.at[src], l_send.at[j], l_recv.at[src],
            device_id=peer(src), device_id_type=MESH,
        ).wait_recv()

    own_slots.wait()
    down_copy.wait()
    slots = slots_in[...].reshape(total_rows, fold_width)
    cols_rank = down_ref.shape[1]
    fold_of = lax.broadcasted_iota(jnp.int32, (total_rows, cols_rank), 0) & 7
    low = jnp.zeros((total_rows, cols_rank), F32)
    for q in range(FOLD):
        term = jnp.dot(
            slots, down_v[q * fold_width:(q + 1) * fold_width, :], preferred_element_type=F32
        )
        low = low + jnp.where(fold_of == q, term, 0.0)
    slot_total = n * capacity
    half = jnp.sum(low.reshape(slot_total, FOLD, cols_rank), axis=1)
    half_out[...] = half
    half_copy = pltpu.make_async_remote_copy(
        half_out, half_in, h_send, h_recv, device_id=partner, device_id_type=MESH
    )
    half_copy.start()

    @pl.loop(1, n)
    def _(j):
        src = (c + j) % n
        pltpu.make_async_remote_copy(
            ids_ref, ids_all.at[src], id_send.at[j], id_recv.at[src], device_id=peer(src),
            device_id_type=MESH,
        ).wait_recv()

    own_ids.wait()
    hit_list, id_list = [], []
    sub = lax.broadcasted_iota(jnp.int32, (row_dev, 128), 0)
    lane = lax.broadcasted_iota(jnp.int32, (row_dev, 128), 1)
    slot_lane = lax.broadcasted_iota(jnp.int32, (row_dev, slot_total), 1).astype(F32)
    me = c.astype(F32)
    for b in range(n):
        id_row = jnp.broadcast_to(ids_all[b, 0:1, 0:128], (row_dev, 128))
        owner_row = jnp.broadcast_to(ids_all[b, 1:2, 0:128], (row_dev, 128))
        id_col = jnp.sum(jnp.where(lane == sub, id_row, 0.0), axis=1, keepdims=True)
        owner_col = jnp.sum(jnp.where(lane == sub, owner_row, 0.0), axis=1, keepdims=True)
        earlier = (owner_row == owner_col) & (lane < sub)
        rank_col = jnp.sum(jnp.where(earlier, 1.0, 0.0), axis=1, keepdims=True)
        slot_col = jnp.where(owner_col == me, b * capacity + rank_col, -1.0)
        hit_list.append(jnp.where(slot_lane == slot_col, 1.0, 0.0))
        id_list.append(jnp.broadcast_to(id_col, (row_dev, cols_rank)))
    hits = jnp.concatenate(hit_list, axis=0).astype(BF16)
    ids = jnp.concatenate(id_list, axis=0)
    half_copy.wait()
    shrink = (half + half_in[...]).astype(BF16)
    spread = jnp.dot(hits, shrink, preferred_element_type=F32)
    first = (lax.broadcasted_iota(jnp.int32, ids.shape, 1) + c * cols_rank).astype(F32)
    off = first - rank * ids
    low_rows = jnp.where((off >= 0.0) & (off < rank), spread * UPDATE_SCALE, 0.0).astype(BF16)

    up_copy.wait()

    def y_copy(k):
        cols = columns(k)
        return pltpu.make_async_remote_copy(
            part.at[1 - yy, :, :, cols], y_in.at[:, :, cols], y_send.at[k], y_recv.at[k],
            device_id=peer(zz * 2 + 1 - yy), device_id_type=MESH,
        )

    @pl.loop(0, chunks)
    def _(k):
        cols = columns(k)
        acc = jnp.dot(low_rows, up_v[:, cols], preferred_element_type=F32)
        for b in range(n):
            one = acc[b * row_dev:(b + 1) * row_dev, :]
            part[b % 2, b // 2, :, cols] = (part[b % 2, b // 2, :, cols].astype(F32) + one).astype(BF16)
        y_copy(k).start()

    def z_copy(k, j):
        to = (zz + j) % m
        cols = columns(k)
        return pltpu.make_async_remote_copy(
            part.at[yy, to, :, cols], z_in.at[zz, :, cols], z_send.at[k, j], z_recv.at[k, zz],
            device_id=peer(to * 2 + yy), device_id_type=MESH,
        )

    @pl.loop(0, chunks)
    def _(k):
        cols = columns(k)
        y_copy(k).wait_recv()
        for b in range(m):
            total = part[yy, b, :, cols].astype(F32) + y_in[b, :, cols].astype(F32)
            part[yy, b, :, cols] = total.astype(BF16)

        @pl.loop(1, m)
        def _(j):
            z_copy(k, j).start()

    @pl.loop(0, chunks)
    def _(k):
        cols = columns(k)
        total = part[yy, zz, :, cols].astype(F32)
        for j in range(1, m):
            src = (zz + j) % m
            pltpu.make_async_remote_copy(
                part.at[yy, src, :, cols], z_in.at[src, :, cols], z_send.at[k, j],
                z_recv.at[k, src], device_id=peer(src * 2 + yy), device_id_type=MESH,
            ).wait_recv()
            total = total + z_in[src, :, cols].astype(F32)
        out_ref[:, cols] = total.astype(out_ref.dtype)

    @pl.loop(0, chunks)
    def _(k):
        y_copy(k).wait_send()

        @pl.loop(1, m)
        def _(j):
            z_copy(k, j).wait_send()

    @pl.loop(1, n)
    def _(j):
        id_copy((c + j) % n, j).wait_send()
        slot_copy((c + j) % n, j).wait_send()

    @pl.loop(0, m)
    def _(j):
        t, copy = tile_copy(j)

        @pl.when(t != c)
        def _():
            copy.wait_send()

    @pl.when(primary)
    def _():
        @pl.loop(0, n)
        def _(src):
            forward(src).wait_send()


def on_device(n, hidden, base, down, up, index):
    row_dev, width = hidden.shape
    tile = base.shape[0]
    per_owner, rank = up.shape[0], up.shape[1]
    joined = per_owner * rank
    down = down.reshape(width, joined)
    up = up.reshape(joined, width)
    capacity = max(2, 2 * row_dev // n)
    chunks = 8
    m = n // 2
    padded = jnp.pad(index, (0, ROW_PAD - row_dev), constant_values=-1)
    owner = jnp.where(padded < 0, -1, padded // per_owner)
    first = (jnp.arange(8) == 0)[:, None]
    ids = jnp.where(first, jnp.tile(padded, FOLD)[None, :], jnp.tile(owner, FOLD)[None, :])
    ids = ids.astype(F32)
    slot_rows = capacity * FOLD
    dma = pltpu.SemaphoreType.DMA
    vmem = pl.BlockSpec(memory_space=pltpu.VMEM)
    anywhere = pl.BlockSpec(memory_space=pl.ANY)
    rows_all = n * row_dev
    return pl.pallas_call(
        functools.partial(kernel, n, capacity, rank, chunks),
        out_shape=jax.ShapeDtypeStruct((row_dev, width), BF16),
        in_specs=[vmem, vmem, anywhere, anywhere, anywhere],
        out_specs=vmem,
        scratch_shapes=[
            pltpu.VMEM((tile, width), BF16),
            pltpu.VMEM((width, joined), BF16),
            pltpu.VMEM((joined, width), BF16),
            pltpu.VMEM((n, 8, FOLD * ROW_PAD), F32),
            pltpu.VMEM((n, row_dev, tile), BF16),
            pltpu.VMEM((rows_all, tile), BF16),
            pltpu.VMEM((FOLD * ROW_PAD, width // FOLD), BF16),
            pltpu.VMEM((n, slot_rows, width // FOLD), BF16),
            pltpu.VMEM((n, slot_rows, width // FOLD), BF16),
            pltpu.VMEM((n * capacity, joined), F32),
            pltpu.VMEM((n * capacity, joined), F32),
            pltpu.VMEM((2, m, row_dev, width), BF16),
            pltpu.VMEM((m, row_dev, width), BF16),
            pltpu.VMEM((m, row_dev, width), BF16),
            dma((chunks,)),
            dma((2,)),
            dma((n,)), dma((n,)),
            dma((m,)), dma((n,)),
            dma((n,)),
            dma((n,)), dma((n,)),
            dma, dma,
            dma((chunks,)), dma((chunks,)),
            dma((chunks, m)), dma((chunks, m)),
        ],
        compiler_params=pltpu.CompilerParams(
            collective_id=0, has_side_effects=True, vmem_limit_bytes=60 * 2**20
        ),
        cost_estimate=pl.CostEstimate(
            flops=2 * rows_all * tile * width, bytes_accessed=2 * tile * width, transcendentals=0
        ),
    )(ids, hidden, base, down, up)


def solution(mesh):
    return jax.shard_map(
        functools.partial(on_device, mesh.shape["gx"]),
        mesh=mesh,
        in_specs=(
            P(("groups", "gx"), "gy"),
            P("gx", "gy"),
            P("gy", "gx", None),
            P("gx", None, "gy"),
            P(("groups", "gx")),
        ),
        out_specs=P(("groups", "gx"), "gy"),
        check_vma=False,
    )
```

time: 184 us -> 92.5 us (0.50)
  waiting for transfers between devices: 113 us -> 0 us
  Pallas kernels: 0 us -> 84.9 us
  matrix products: 24.9 us -> 0 us
  starting transfers between devices: 18.4 us -> 0 us
  between operations: 13.5 us -> 0.01 us
  blocking collectives: 5.66 us -> 0 us
    pallas_call x0 -> x1, Pallas kernels: none -> 84.9 us  [on_device(): pl.pallas_call(functools.partial(kernel, n, capacity, rank, chunks), out_...]
    reduce_scatter x1 -> x0, waiting for transfers between devices: 73.5 us -> none  [on_device(): lax.psum_scatter((lax.optimization_barrier(partial_sum).astype(jnp.float3...]
    all_to_all x4 -> x0, waiting for transfers between devices: 39.7 us -> none  [the longest x1 20.2 us: on_device(): lax.all_to_all(payload[0], 'gx', split_axis=0, concat_axis=0, tiled=True)]
    dot_general x4 -> x0, matrix products: 24.9 us -> none  [the longest x1 16 us: on_device(): jnp.dot(tile_rows, base_projection_weight, preferred_element_type=jnp.flo...]
    all_to_all x4 -> x0, starting transfers between devices: 18.4 us -> none  [the longest x1 7.28 us: on_device(): lax.all_to_all(payload[2], 'gx', split_axis=0, concat_axis=0, tiled=True)]
    psum x1 -> x0, blocking collectives: 3.29 us -> none  [on_device(): lax.psum(jnp.dot(flat_rows, down_joined_weight, preferred_element_type=jn...]
    all_gather x1 -> x0, blocking collectives: 2.37 us -> none  [on_device(): full_rows = lax.all_gather(hidden_state_rows, 'gy', axis=1, tiled=True)]
    reshape x2 -> x1, local copies, waits for them, and re-layouts: 2.45 us -> 4.09 us  [on_device(): down = down.reshape(width, joined)]
  transfers between devices with their start and end apart: 5 -> 0, of which waited for: 5 -> 0; matrix products, arithmetic and copies ran while one was open for 5% -> 0% of each run, Pallas kernels for 0% -> 0%
where the time goes in v1:
time: 92.5 us; the launch traced here: 92.3 us
  Pallas kernels  84.9 us (92%)
  local copies, waits for them, and re-layouts  6.02 us (7%)
  other arithmetic  1.34 us (1%)
    pallas_call x1, Pallas kernels, on_device(): pl.pallas_call(functools.partial(kernel, n, capacity, rank, chunks), out_...  84.9 us
    reshape x1, local copies, waits for them, and re-layouts, on_device(): down = down.reshape(width, joined)  4.09 us

profile of v1, /device:TPU:0, one launch (start us, length us, event | category | flops | bytes accessed | tf_op | source)
XLA Modules:
  0.0 92.3 jit_solution(11942815091285052492)
XLA Ops:
  0.0 0.7 fusion.1
  0.7 0.1 broadcast_in_dim.34
  0.8 0.1 broadcast_in_dim.37
  0.8 0.7 select_convert_fusion.ids_ref
  1.5 4.1 %copy.7.down_ref = bf16[8192,128]{1,0:T(8,128)(2,1)} copy(bf16[8192,128]{0,1:T(8,128)(2,1)} %bitcast.2) | data formatting | bytes 4194304 | tf_op jit(solution)/shard_map/reshape | solution.py:309
  5.6 84.9 %shard_map.55 = bf16[24,8192]{1,0:T(8,128)(2,1)} custom-call(f32[8,256]{1,0:T(8,128)} %select_convert_fusion.ids_ref, bf16[24,8192]{1,0:T(8,128)(2,1)} %hid_ref.1, bf16[2048,8192]{1,0:T(8,128)(2,1)} %w_ref.1, bf16[8192,128]{1,0:T(8,128)(2,1)} %copy.7.down_ref, bf16[128,8192]{1,0:T(8,128)(2,1)} %bitcast.3), custom_call_target="tpu_custom_call" | custom-call | flops 6442450944 | bytes 33554432 | tf_op jit(solution)/shard_map/pallas_call | solution.py:324
  90.5 1.8 %copy.9 = bf16[24,8192]{1,0:T(8,128)(2,1)} copy(bf16[24,8192]{1,0:T(8,128)(2,1)} %shard_map.55) | data formatting | bytes 786432
  (3 shorter events, 0.0 us)

commit v2 on v1

--- a/solution.py
+++ b/solution.py
@@ -19,9 +19,9 @@
     n, capacity, rank, chunks,
     ids_ref, hid_ref, w_ref, down_ref, up_ref, out_ref,
     w_v, down_v, up_v, ids_all, tile_in, rows, folded, packed, slots_in,
-    half_out, half_in, part, y_in, z_in,
+    half_out, half_in, part, y_in, z_in, low_slots, d_own, d_out, d_in,
     w_sem, ad_sem, id_send, id_recv, t_send, t_recv, f_send, l_send, l_recv,
-    h_send, h_recv, y_send, y_recv, z_send, z_recv,
+    h_send, h_recv, y_send, y_recv, z_send, z_recv, d_send, d_recv,
 ):
     g, c, s = lax.axis_index("groups"), lax.axis_index("gx"), lax.axis_index("gy")
     m = n // 2
@@ -125,6 +125,14 @@
             device_id_type=MESH,
         )
 
+    @pl.loop(0, m)
+    def _(j):
+        t, copy = tile_copy(j)
+
+        @pl.when(t != c)
+        def _():
+            copy.wait_send()
+
     @pl.loop(1, n)
     def _(j):
         slot_copy((c + j) % n, j).start()
@@ -154,6 +162,15 @@
     def columns(k):
         return pl.ds(pl.multiple_of(k * cc, cc), cc)
 
+    def y_copy(k):
+        cols = columns(k)
+        return pltpu.make_async_remote_copy(
+            part.at[1 - yy, :, :, cols], y_in.at[:, :, cols], y_send.at[k], y_recv.at[k],
+            device_id=peer(zz * 2 + 1 - yy), device_id_type=MESH,
+        )
+
+    early = chunks // 2
+
     @pl.loop(0, chunks)
     def _(k):
         w_copy(k).wait()
@@ -161,6 +178,10 @@
         acc = jnp.dot(rows[...], w_v[:, cols], preferred_element_type=F32)
         for b in range(n):
             part[b % 2, b // 2, :, cols] = acc[b * row_dev:(b + 1) * row_dev, :].astype(BF16)
+
+        @pl.when(k < early)
+        def _():
+            y_copy(k).start()
 
     @pl.loop(1, n)
     def _(j):
@@ -173,12 +194,13 @@
     own_slots.wait()
     down_copy.wait()
     slots = slots_in[...].reshape(total_rows, fold_width)
-    cols_rank = down_ref.shape[1]
+    cols_rank = down_ref.shape[0]
     fold_of = lax.broadcasted_iota(jnp.int32, (total_rows, cols_rank), 0) & 7
     low = jnp.zeros((total_rows, cols_rank), F32)
     for q in range(FOLD):
-        term = jnp.dot(
-            slots, down_v[q * fold_width:(q + 1) * fold_width, :], preferred_element_type=F32
+        term = lax.dot_general(
+            slots, down_v[:, q * fold_width:(q + 1) * fold_width], (((1,), (1,)), ((), ())),
+            preferred_element_type=F32,
         )
         low = low + jnp.where(fold_of == q, term, 0.0)
     slot_total = n * capacity
@@ -198,21 +220,40 @@
         ).wait_recv()
 
     own_ids.wait()
-    hit_list, id_list = [], []
     sub = lax.broadcasted_iota(jnp.int32, (row_dev, 128), 0)
     lane = lax.broadcasted_iota(jnp.int32, (row_dev, 128), 1)
-    slot_lane = lax.broadcasted_iota(jnp.int32, (row_dev, slot_total), 1).astype(F32)
-    me = c.astype(F32)
-    for b in range(n):
+    side = m * capacity
+
+    def slot_of(b):
         id_row = jnp.broadcast_to(ids_all[b, 0:1, 0:128], (row_dev, 128))
         owner_row = jnp.broadcast_to(ids_all[b, 1:2, 0:128], (row_dev, 128))
         id_col = jnp.sum(jnp.where(lane == sub, id_row, 0.0), axis=1, keepdims=True)
         owner_col = jnp.sum(jnp.where(lane == sub, owner_row, 0.0), axis=1, keepdims=True)
         earlier = (owner_row == owner_col) & (lane < sub)
         rank_col = jnp.sum(jnp.where(earlier, 1.0, 0.0), axis=1, keepdims=True)
-        slot_col = jnp.where(owner_col == me, b * capacity + rank_col, -1.0)
+        return id_col, owner_col, rank_col
+
+    me = c.astype(F32)
+    other = (zz * 2 + 1 - yy).astype(F32)
+    slot_lane = lax.broadcasted_iota(jnp.int32, (row_dev, slot_total), 1).astype(F32)
+    side_lane = lax.broadcasted_iota(jnp.int32, (row_dev, side), 1).astype(F32)
+    hit_list, id_list, side_list, own_list, other_list = [], [], [], [], []
+    for b in range(n):
+        id_col, owner_col, rank_col = slot_of(b)
+        mine = owner_col == me
+        slot_col = jnp.where(mine, b * capacity + rank_col, -1.0)
         hit_list.append(jnp.where(slot_lane == slot_col, 1.0, 0.0))
+        slot_col = jnp.where(mine, (b % 2) * side + (b // 2) * capacity + rank_col, -1.0)
+        side_list.append(jnp.where(slot_lane == slot_col, 1.0, 0.0))
         id_list.append(jnp.broadcast_to(id_col, (row_dev, cols_rank)))
+    for b in range(m):
+        id_col, owner_col, rank_col = slot_of(2 * b + yy)
+        at = b * capacity + rank_col
+        own_list.append(jnp.where(side_lane == jnp.where(owner_col == me, at, -1.0), 1.0, 0.0))
+        other_list.append(jnp.where(side_lane == jnp.where(owner_col == other, at, -1.0), 1.0, 0.0))
+    sides = jnp.concatenate(side_list, axis=0).astype(BF16)
+    own_hits = jnp.concatenate(own_list, axis=0).astype(BF16)
+    other_hits = jnp.concatenate(other_list, axis=0).astype(BF16)
     hits = jnp.concatenate(hit_list, axis=0).astype(BF16)
     ids = jnp.concatenate(id_list, axis=0)
     half_copy.wait()
@@ -222,23 +263,36 @@
     off = first - rank * ids
     low_rows = jnp.where((off >= 0.0) & (off < rank), spread * UPDATE_SCALE, 0.0).astype(BF16)
 
+    by_side = lax.dot_general(
+        sides, low_rows, (((0,), (0,)), ((), ())), preferred_element_type=F32
+    )
+    for y in range(2):
+        low_slots[y] = by_side[y * side:(y + 1) * side, :].astype(BF16)
+
     up_copy.wait()
 
-    def y_copy(k):
-        cols = columns(k)
-        return pltpu.make_async_remote_copy(
-            part.at[1 - yy, :, :, cols], y_in.at[:, :, cols], y_send.at[k], y_recv.at[k],
+    def d_copy(k):
+        cols = columns(k)
+        return pltpu.make_async_remote_copy(
+            d_out.at[:, cols], d_in.at[:, cols], d_send.at[k], d_recv.at[k],
             device_id=peer(zz * 2 + 1 - yy), device_id_type=MESH,
         )
 
     @pl.loop(0, chunks)
     def _(k):
         cols = columns(k)
-        acc = jnp.dot(low_rows, up_v[:, cols], preferred_element_type=F32)
-        for b in range(n):
-            one = acc[b * row_dev:(b + 1) * row_dev, :]
-            part[b % 2, b // 2, :, cols] = (part[b % 2, b // 2, :, cols].astype(F32) + one).astype(BF16)
-        y_copy(k).start()
+        d_out[:, cols] = jnp.dot(
+            low_slots[1 - yy], up_v[:, cols], preferred_element_type=F32
+        ).astype(BF16)
+        d_copy(k).start()
+
+        @pl.when(k % 2 == 1)
+        def _():
+            y_copy(early + k // 2).start()
+
+        d_own[:, cols] = jnp.dot(
+            low_slots[yy], up_v[:, cols], preferred_element_type=F32
+        ).astype(BF16)
 
     def z_copy(k, j):
         to = (zz + j) % m
@@ -252,8 +306,12 @@
     def _(k):
         cols = columns(k)
         y_copy(k).wait_recv()
+        d_copy(k).wait_recv()
+        delta = jnp.dot(own_hits, d_own[:, cols], preferred_element_type=F32)
+        delta = delta + jnp.dot(other_hits, d_in[:, cols], preferred_element_type=F32)
         for b in range(m):
             total = part[yy, b, :, cols].astype(F32) + y_in[b, :, cols].astype(F32)
+            total = total + delta[b * row_dev:(b + 1) * row_dev, :]
             part[yy, b, :, cols] = total.astype(BF16)
 
         @pl.loop(1, m)
@@ -276,6 +334,7 @@
     @pl.loop(0, chunks)
     def _(k):
         y_copy(k).wait_send()
+        d_copy(k).wait_send()
 
         @pl.loop(1, m)
         def _(j):
@@ -285,14 +344,6 @@
     def _(j):
         id_copy((c + j) % n, j).wait_send()
         slot_copy((c + j) % n, j).wait_send()
-
-    @pl.loop(0, m)
-    def _(j):
-        t, copy = tile_copy(j)
-
-        @pl.when(t != c)
-        def _():
-            copy.wait_send()
 
     @pl.when(primary)
     def _():
@@ -306,10 +357,10 @@
     tile = base.shape[0]
     per_owner, rank = up.shape[0], up.shape[1]
     joined = per_owner * rank
-    down = down.reshape(width, joined)
+    down = down.transpose(1, 2, 0).reshape(joined, width)
     up = up.reshape(joined, width)
     capacity = max(2, 2 * row_dev // n)
-    chunks = 8
+    chunks = 16
     m = n // 2
     padded = jnp.pad(index, (0, ROW_PAD - row_dev), constant_values=-1)
     owner = jnp.where(padded < 0, -1, padded // per_owner)
@@ -328,7 +379,7 @@
         out_specs=vmem,
         scratch_shapes=[
             pltpu.VMEM((tile, width), BF16),
-            pltpu.VMEM((width, joined), BF16),
+            pltpu.VMEM((joined, width), BF16),
             pltpu.VMEM((joined, width), BF16),
             pltpu.VMEM((n, 8, FOLD * ROW_PAD), F32),
             pltpu.VMEM((n, row_dev, tile), BF16),
@@ -341,6 +392,10 @@
             pltpu.VMEM((2, m, row_dev, width), BF16),
             pltpu.VMEM((m, row_dev, width), BF16),
             pltpu.VMEM((m, row_dev, width), BF16),
+            pltpu.VMEM((2, m * capacity, joined), BF16),
+            pltpu.VMEM((m * capacity, width), BF16),
+            pltpu.VMEM((m * capacity, width), BF16),
+            pltpu.VMEM((m * capacity, width), BF16),
             dma((chunks,)),
             dma((2,)),
             dma((n,)), dma((n,)),
@@ -350,6 +405,7 @@
             dma, dma,
             dma((chunks,)), dma((chunks,)),
             dma((chunks, m)), dma((chunks, m)),
+            dma((chunks,)), dma((chunks,)),
         ],
         compiler_params=pltpu.CompilerParams(
             collective_id=0, has_side_effects=True, vmem_limit_bytes=60 * 2**20

time: 92.5 us -> 89.5 us (0.968)
  the two profiles are of different devices: /device:TPU:0 before, /device:TPU:25 now
where the time goes in v2:
time: 89.5 us; the launch traced here: 89.3 us
  Pallas kernels  86 us (96%)
  local copies, waits for them, and re-layouts  1.93 us (2%)
  other arithmetic  1.34 us (1%)
    pallas_call x1, Pallas kernels, on_device(): pl.pallas_call(functools.partial(kernel, n, capacity, rank, chunks), out_...  86 us

profile of v2, /device:TPU:25, one launch (start us, length us, event | category | flops | bytes accessed | tf_op | source)
XLA Modules:
  0.0 89.3 jit_solution(7643598658976425853)
XLA Ops:
  0.0 0.7 fusion.1
  0.7 0.1 broadcast_in_dim.34
  0.8 0.1 broadcast_in_dim.37
  0.8 0.7 select_convert_fusion.ids_ref
  1.5 86.0 %shard_map.55 = bf16[24,8192]{1,0:T(8,128)(2,1)} custom-call(f32[8,256]{1,0:T(8,128)} %select_convert_fusion.ids_ref, bf16[24,8192]{1,0:T(8,128)(2,1)} %hid_ref.1, bf16[2048,8192]{1,0:T(8,128)(2,1)} %w_ref.1, bf16[128,8192]{1,0:T(8,128)(2,1)} %bitcast.4, bf16[128,8192]{1,0:T(8,128)(2,1)} %bitcast.5), custom_call_target="tpu_custom_call" | custom-call | flops 6442450944 | bytes 33554432 | tf_op jit(solution)/shard_map/pallas_call | solution.py:375
  87.5 1.8 %copy.7 = bf16[24,8192]{1,0:T(8,128)(2,1)} copy(bf16[24,8192]{1,0:T(8,128)(2,1)} %shard_map.55) | data formatting | bytes 786432
  (3 shorter events, 0.0 us)

commit v3 on v2

--- a/solution.py
+++ b/solution.py
@@ -19,9 +19,9 @@
     n, capacity, rank, chunks,
     ids_ref, hid_ref, w_ref, down_ref, up_ref, out_ref,
     w_v, down_v, up_v, ids_all, tile_in, rows, folded, packed, slots_in,
-    half_out, half_in, part, y_in, z_in, low_slots, d_own, d_out, d_in,
+    half_out, half_in, part, y_in, up_in, dn_in, low_slots, d_own, d_out, d_in,
     w_sem, ad_sem, id_send, id_recv, t_send, t_recv, f_send, l_send, l_recv,
-    h_send, h_recv, y_send, y_recv, z_send, z_recv, d_send, d_recv,
+    h_send, h_recv, y_send, y_recv, u_send, u_recv, n_send, n_recv, d_send, d_recv,
 ):
     g, c, s = lax.axis_index("groups"), lax.axis_index("gx"), lax.axis_index("gy")
     m = n // 2
@@ -294,51 +294,105 @@
             low_slots[yy], up_v[:, cols], preferred_element_type=F32
         ).astype(BF16)
 
-    def z_copy(k, j):
-        to = (zz + j) % m
-        cols = columns(k)
-        return pltpu.make_async_remote_copy(
-            part.at[yy, to, :, cols], z_in.at[zz, :, cols], z_send.at[k, j], z_recv.at[k, zz],
-            device_id=peer(to * 2 + yy), device_id_type=MESH,
-        )
+    def z_copy(k, b, step, buffer, send, recv):
+        cols = columns(k)
+        return pltpu.make_async_remote_copy(
+            buffer.at[b, :, cols], buffer.at[b, :, cols], send.at[k, b], recv.at[k, b],
+            device_id=peer((zz + step + m) % m * 2 + yy), device_id_type=MESH,
+        )
+
+    def up_copy_of(k, b):
+        return z_copy(k, b, 1, up_in, u_send, u_recv)
+
+    def dn_copy_of(k, b):
+        return z_copy(k, b, -1, dn_in, n_send, n_recv)
+
+    def pass_on(k, b, copy_of, buffer, starts):
+        cols = columns(k)
+        own = part[yy, b, :, cols]
+
+        @pl.when(starts)
+        def _():
+            buffer[b, :, cols] = own
+
+        @pl.when(jnp.logical_not(starts))
+        def _():
+            copy_of(k, b).wait_recv()
+            total = own.astype(F32) + buffer[b, :, cols].astype(F32)
+            buffer[b, :, cols] = total.astype(BF16)
+
+        copy_of(k, b).start()
+
+    lag = 2
+
+    @pl.loop(0, chunks + lag * (m - 1))
+    def _(i):
+        @pl.when(i < chunks)
+        def _():
+            cols = columns(i)
+            y_copy(i).wait_recv()
+            d_copy(i).wait_recv()
+            delta = jnp.dot(own_hits, d_own[:, cols], preferred_element_type=F32)
+            delta = delta + jnp.dot(other_hits, d_in[:, cols], preferred_element_type=F32)
+            for b in range(m):
+                total = part[yy, b, :, cols].astype(F32) + y_in[b, :, cols].astype(F32)
+                total = total + delta[b * row_dev:(b + 1) * row_dev, :]
+                part[yy, b, :, cols] = total.astype(BF16)
+
+        k_up = i - lag * zz
+
+        @pl.when((k_up >= 0) & (k_up < chunks))
+        def _():
+            @pl.loop(zz + 1, m)
+            def _(b):
+                pass_on(k_up, b, up_copy_of, up_in, zz == 0)
+
+        k_dn = i - lag * (m - 1 - zz)
+
+        @pl.when((k_dn >= 0) & (k_dn < chunks))
+        def _():
+            @pl.loop(0, zz)
+            def _(b):
+                pass_on(k_dn, b, dn_copy_of, dn_in, zz == m - 1)
 
     @pl.loop(0, chunks)
     def _(k):
         cols = columns(k)
-        y_copy(k).wait_recv()
-        d_copy(k).wait_recv()
-        delta = jnp.dot(own_hits, d_own[:, cols], preferred_element_type=F32)
-        delta = delta + jnp.dot(other_hits, d_in[:, cols], preferred_element_type=F32)
-        for b in range(m):
-            total = part[yy, b, :, cols].astype(F32) + y_in[b, :, cols].astype(F32)
-            total = total + delta[b * row_dev:(b + 1) * row_dev, :]
-            part[yy, b, :, cols] = total.astype(BF16)
-
-        @pl.loop(1, m)
-        def _(j):
-            z_copy(k, j).start()
-
-    @pl.loop(0, chunks)
-    def _(k):
-        cols = columns(k)
-        total = part[yy, zz, :, cols].astype(F32)
-        for j in range(1, m):
-            src = (zz + j) % m
-            pltpu.make_async_remote_copy(
-                part.at[yy, src, :, cols], z_in.at[src, :, cols], z_send.at[k, j],
-                z_recv.at[k, src], device_id=peer(src * 2 + yy), device_id_type=MESH,
-            ).wait_recv()
-            total = total + z_in[src, :, cols].astype(F32)
-        out_ref[:, cols] = total.astype(out_ref.dtype)
+        own = part[yy, zz, :, cols].astype(F32)
+
+        @pl.when(zz > 0)
+        def _():
+            up_copy_of(k, zz).wait_recv()
+
+        @pl.when(zz < m - 1)
+        def _():
+            dn_copy_of(k, zz).wait_recv()
+
+        @pl.when(zz == 0)
+        def _():
+            out_ref[:, cols] = (own + dn_in[zz, :, cols].astype(F32)).astype(BF16)
+
+        @pl.when(zz == m - 1)
+        def _():
+            out_ref[:, cols] = (own + up_in[zz, :, cols].astype(F32)).astype(BF16)
+
+        @pl.when((zz > 0) & (zz < m - 1))
+        def _():
+            total = own + dn_in[zz, :, cols].astype(F32) + up_in[zz, :, cols].astype(F32)
+            out_ref[:, cols] = total.astype(BF16)
 
     @pl.loop(0, chunks)
     def _(k):
         y_copy(k).wait_send()
         d_copy(k).wait_send()
 
-        @pl.loop(1, m)
-        def _(j):
-            z_copy(k, j).wait_send()
+        @pl.loop(zz + 1, m)
+        def _(b):
+            up_copy_of(k, b).wait_send()
+
+        @pl.loop(0, zz)
+        def _(b):
+            dn_copy_of(k, b).wait_send()
 
     @pl.loop(1, n)
     def _(j):
@@ -392,6 +446,7 @@
             pltpu.VMEM((2, m, row_dev, width), BF16),
             pltpu.VMEM((m, row_dev, width), BF16),
             pltpu.VMEM((m, row_dev, width), BF16),
+            pltpu.VMEM((m, row_dev, width), BF16),
             pltpu.VMEM((2, m * capacity, joined), BF16),
             pltpu.VMEM((m * capacity, width), BF16),
             pltpu.VMEM((m * capacity, width), BF16),
@@ -404,6 +459,7 @@
             dma((n,)), dma((n,)),
             dma, dma,
             dma((chunks,)), dma((chunks,)),
+            dma((chunks, m)), dma((chunks, m)),
             dma((chunks, m)), dma((chunks, m)),
             dma((chunks,)), dma((chunks,)),
         ],

time: 89.5 us -> 93.2 us (1.041)
  the two profiles are of different devices: /device:TPU:25 before, /device:TPU:0 now
where the time goes in v3:
time: 93.2 us; the launch traced here: 92.9 us
  Pallas kernels  89.7 us (96%)
  local copies, waits for them, and re-layouts  1.93 us (2%)
  other arithmetic  1.34 us (1%)
    pallas_call x1, Pallas kernels, on_device(): pl.pallas_call(functools.partial(kernel, n, capacity, rank, chunks), out_...  89.7 us

profile of v3, /device:TPU:0, one launch (start us, length us, event | category | flops | bytes accessed | tf_op | source)
XLA Modules:
  0.0 92.9 jit_solution(13857397591628203978)
XLA Ops:
  0.0 0.7 fusion.1
  0.7 0.1 broadcast_in_dim.34
  0.8 0.1 broadcast_in_dim.37
  0.8 0.7 select_convert_fusion.ids_ref
  1.5 89.7 %shard_map.55 = bf16[24,8192]{1,0:T(8,128)(2,1)} custom-call(f32[8,256]{1,0:T(8,128)} %select_convert_fusion.ids_ref, bf16[24,8192]{1,0:T(8,128)(2,1)} %hid_ref.1, bf16[2048,8192]{1,0:T(8,128)(2,1)} %w_ref.1, bf16[128,8192]{1,0:T(8,128)(2,1)} %bitcast.4, bf16[128,8192]{1,0:T(8,128)(2,1)} %bitcast.5), custom_call_target="tpu_custom_call" | custom-call | flops 6442450944 | bytes 33554432 | tf_op jit(solution)/shard_map/pallas_call | solution.py:429
  91.2 1.8 %copy.7 = bf16[24,8192]{1,0:T(8,128)(2,1)} copy(bf16[24,8192]{1,0:T(8,128)(2,1)} %shard_map.55) | data formatting | bytes 786432
  (3 shorter events, 0.0 us)

commit v4 on v1

--- a/solution.py
+++ b/solution.py
@@ -125,6 +125,14 @@
             device_id_type=MESH,
         )
 
+    @pl.loop(0, m)
+    def _(j):
+        t, copy = tile_copy(j)
+
+        @pl.when(t != c)
+        def _():
+            copy.wait_send()
+
     @pl.loop(1, n)
     def _(j):
         slot_copy((c + j) % n, j).start()
@@ -173,12 +181,13 @@
     own_slots.wait()
     down_copy.wait()
     slots = slots_in[...].reshape(total_rows, fold_width)
-    cols_rank = down_ref.shape[1]
+    cols_rank = down_ref.shape[0]
     fold_of = lax.broadcasted_iota(jnp.int32, (total_rows, cols_rank), 0) & 7
     low = jnp.zeros((total_rows, cols_rank), F32)
     for q in range(FOLD):
-        term = jnp.dot(
-            slots, down_v[q * fold_width:(q + 1) * fold_width, :], preferred_element_type=F32
+        term = lax.dot_general(
+            slots, down_v[:, q * fold_width:(q + 1) * fold_width], (((1,), (1,)), ((), ())),
+            preferred_element_type=F32,
         )
         low = low + jnp.where(fold_of == q, term, 0.0)
     slot_total = n * capacity
@@ -286,14 +295,6 @@
         id_copy((c + j) % n, j).wait_send()
         slot_copy((c + j) % n, j).wait_send()
 
-    @pl.loop(0, m)
-    def _(j):
-        t, copy = tile_copy(j)
-
-        @pl.when(t != c)
-        def _():
-            copy.wait_send()
-
     @pl.when(primary)
     def _():
         @pl.loop(0, n)
@@ -306,7 +307,7 @@
     tile = base.shape[0]
     per_owner, rank = up.shape[0], up.shape[1]
     joined = per_owner * rank
-    down = down.reshape(width, joined)
+    down = down.transpose(1, 2, 0).reshape(joined, width)
     up = up.reshape(joined, width)
     capacity = max(2, 2 * row_dev // n)
     chunks = 8
@@ -328,7 +329,7 @@
         out_specs=vmem,
         scratch_shapes=[
             pltpu.VMEM((tile, width), BF16),
-            pltpu.VMEM((width, joined), BF16),
+            pltpu.VMEM((joined, width), BF16),
             pltpu.VMEM((joined, width), BF16),
             pltpu.VMEM((n, 8, FOLD * ROW_PAD), F32),
             pltpu.VMEM((n, row_dev, tile), BF16),

time: 92.5 us -> 88 us (0.951)
  local copies, waits for them, and re-layouts: 6.02 us -> 1.93 us
    reshape x1 -> x0, local copies, waits for them, and re-layouts: 4.09 us -> none  [on_device(): down = down.reshape(width, joined)]
where the time goes in v4:
time: 88 us; the launch traced here: 87.8 us
  Pallas kernels  84.5 us (96%)
  local copies, waits for them, and re-layouts  1.93 us (2%)
  other arithmetic  1.34 us (2%)
    pallas_call x1, Pallas kernels, on_device(): pl.pallas_call(functools.partial(kernel, n, capacity, rank, chunks), out_...  84.5 us
    unnamed x1, local copies, waits for them, and re-layouts  1.77 us

profile of v4, /device:TPU:0, one launch (start us, length us, event | category | flops | bytes accessed | tf_op | source)
XLA Modules:
  0.0 87.8 jit_solution(18084848444089893040)
XLA Ops:
  0.0 0.7 fusion.1
  0.7 0.1 broadcast_in_dim.34
  0.8 0.1 broadcast_in_dim.37
  0.8 0.7 select_convert_fusion.ids_ref
  1.5 84.5 %shard_map.55 = bf16[24,8192]{1,0:T(8,128)(2,1)} custom-call(f32[8,256]{1,0:T(8,128)} %select_convert_fusion.ids_ref, bf16[24,8192]{1,0:T(8,128)(2,1)} %hid_ref.1, bf16[2048,8192]{1,0:T(8,128)(2,1)} %w_ref.1, bf16[128,8192]{1,0:T(8,128)(2,1)} %bitcast.4, bf16[128,8192]{1,0:T(8,128)(2,1)} %bitcast.5), custom_call_target="tpu_custom_call" | custom-call | flops 6442450944 | bytes 33554432 | tf_op jit(solution)/shard_map/pallas_call | solution.py:325
  86.0 1.8 %copy.7 = bf16[24,8192]{1,0:T(8,128)(2,1)} copy(bf16[24,8192]{1,0:T(8,128)(2,1)} %shard_map.55) | data formatting | bytes 786432
  (3 shorter events, 0.0 us)
